TPU v7x, 128 devices: a whole 4x4x4 slice. The times are simulated.
128 devices in a mesh: wave: 32 (over z, x, core), fld: 4 (over y).
Axes of the slice: x: 4, y: 4, z: 4, core: 2. Of those that a mesh axis runs over, the one named last changes fastest.
Arguments:
- spec_in: bfloat16 [24, 1280, 2, 1280], P('fld', 'wave'), may hold values from -16 to 16
- legendre: bfloat16 [1280, 512, 1280], P('wave', 'fld'), may hold values from -0.15625 to 0.15625
- wave_order: int32 [1280], replicated, may hold values from 0 to 1279, as said below
- row_length: int32 [512], replicated, may hold values from 512 to 5632, as said below
- quad_weight: float32 [512], replicated, may hold values from 0.5 to 2
- mixing: float32 [24, 24], replicated, may hold values from -1.25 to 1.25
- square_gain: float32 [24], replicated, may hold values from 0.5 to 1
Outputs:
- spec_out: float32 [24, 1280, 2, 1280], P('fld', 'wave')
Inputs may be any that keep to these rules, and one draw needn't show every extreme that they name: `wave_order`: A permutation of the wavenumbers in which rows 2k and 2k + 1 hold a wavenumber m and 1279 - m. `row_length`: each value is 20 + 4 i for an octahedral row index i below 1280, rounded up to a multiple of 512; one latitude has 5632.
All inputs are finite; a program needn't handle non-finite values.
Results may differ from a plain program's by a relative error of at most 0.0054.
Values may be sent and summed in bfloat16 or wider, within the bound.
A program may use at most 192 MiB of HBM per device.

v0:
```python
import functools
import math

import jax
import jax.numpy as jnp
import numpy as np
from jax import lax
from jax.experimental import pallas as pl
from jax.experimental.pallas import tpu as pltpu
from jax.sharding import PartitionSpec as P

M = 1280
FL = 24
BLOCK = 512
LANES = 128
NB = M // LANES
PB = NB + 1
PACKED = PB * LANES
CHUNKS = 5
PAIRS = 4
WAVE = 32
FLD = 4
LATS = 4
FD = FL // FLD
ROWS = 2 * FD * PAIRS
HALF = BLOCK // 2
EVEN = HALF + 16
XMAX = 12
F32, BF16, I32 = jnp.float32, jnp.bfloat16, jnp.int32


def wave_tables():
    v = np.arange(BLOCK)
    angle = (v[:, None] * v[None, :] % BLOCK) * (2.0 * math.pi / BLOCK)
    return np.concatenate([np.cos(angle), -np.sin(angle)], axis=1).astype(np.float32)


def lane_maps():
    width = LATS * LANES
    lat_a, ab_a, level_a, half_a = (np.full(width, -1) for _ in range(4))
    for lat in range(LATS):
        for ab in range(2):
            for g in range(FLD):
                for c in range(2):
                    for f in range(FD):
                        at = LANES * lat + ((ab * FLD + g) * 2 + c) * FD + f
                        lat_a[at], ab_a[at], half_a[at], level_a[at] = lat, ab, c, FD * g + f
    lat_b, ab_b, level_b, half_b = (np.full(width, -2) for _ in range(4))
    for c in range(2):
        for ab in range(2):
            for lat in range(LATS):
                for f in range(FL):
                    at = LANES * (2 * c + ab) + FL * lat + f
                    lat_b[at], ab_b[at], half_b[at], level_b[at] = lat, ab, c, f
    same = (
        (lat_a[:, None] == lat_b[None, :])
        & (ab_a[:, None] == ab_b[None, :])
        & (half_a[:, None] == half_b[None, :])
    )
    pick = same & (level_a[:, None] == level_b[None, :])
    return pick.T.astype(np.float32)


def turn_pair(t):
    a = (t - 0.25) * (2.0 * math.pi)
    s = a * a
    sine = a * (
        1.0
        + s
        * (
            -1.0 / 6
            + s * (1.0 / 120 + s * (-1.0 / 5040 + s * (1.0 / 362880 - s * (1.0 / 39916800))))
        )
    )
    cosine = 1.0 + s * (
        -0.5
        + s
        * (
            1.0 / 24
            + s * (-1.0 / 720 + s * (1.0 / 40320 + s * (-1.0 / 3628800 + s * (1.0 / 479001600))))
        )
    )
    return -sine, cosine


def times(a, b):
    return a[0] * b[0] - a[1] * b[1], a[0] * b[1] + a[1] * b[0]


def back(a, b):
    return a[0] * b[0] + a[1] * b[1], a[1] * b[0] - a[0] * b[1]


SENT = NB * ROWS + 16
LEFT_PART = SENT // 32 * 16
GROUP = 8
MESH = pl.DeviceIdType.MESH
OTHERS = sorted(
    ((dz, dx, dc) for dz in range(4) for dx in range(4) for dc in range(2) if dz + dx + dc > 0),
    key=lambda d: -(min(d[0], 4 - d[0]) + min(d[1], 4 - d[1])),
)


def load_packed(leg_ref, packed_ref, first, q):
    q = jnp.broadcast_to(q.astype(F32), (LANES, LANES)).astype(BF16)
    spare = None
    for t in range(NB):
        one = leg_ref[first, :, LANES * t : LANES * (t + 1)]
        at = NB - 1 - t
        two = leg_ref[first + 1, :, LANES * at : LANES * (at + 1)]
        packed_ref[:, LANES * t : LANES * (t + 1)] = jnp.where(q <= t, one, two)
        spare = two if t == 0 else jnp.where(q == t, two, spare)
    packed_ref[:, LANES * NB :] = spare


def kernel(
    spec_ref, leg_ref, fixed_ref, own_ref, lengths_ref, weights_ref, gains_ref,
    order_ref, mixing_ref, out_ref,
    legs, base_ref, pick_ref, turn_ref, spec, rows, orders, mix_ref, column_orders,
    gathered, coeff, flipped, packed, wide, turn, sent, arrived, table, turned, waves, grid, update, edge,
    tr, ti, sent_back, arrived_back, opposite, part_right, part_left, part_own, to_right, to_left,
    first_left, first_right, second_left, second_right, results,
    leg_sem, spec_sem, const_sem, out_sem, ag_send, ag_recv, a_send, a_recv, b_send, b_recv,
    rs_send, rs_recv,
):
    w = lax.axis_index("wave")
    g = lax.axis_index("fld")
    right, left, across = lax.rem(g + 1, FLD), lax.rem(g + 3, FLD), lax.rem(g + 2, FLD)

    def spec_copy(k):
        return pltpu.make_async_copy(
            spec_ref.at[:, pl.ds(k * GROUP, GROUP)], spec.at[k], spec_sem.at[k]
        )

    def out_copy(k):
        return pltpu.make_async_copy(
            results.at[k], out_ref.at[:, pl.ds(k * GROUP, GROUP)], out_sem.at[k]
        )

    fixed_copy = pltpu.make_async_copy(fixed_ref, grid.at[:, pl.ds(0, BLOCK)], const_sem)

    def leg_copy(k):
        rows = pl.ds(k * GROUP, GROUP)
        return pltpu.make_async_copy(leg_ref.at[rows], legs.at[rows], leg_sem.at[k])

    def remote(src, dst, send, recv, to):
        return pltpu.make_async_remote_copy(
            src_ref=src, dst_ref=dst, send_sem=send, recv_sem=recv, device_id=to, device_id_type=MESH
        )

    to_r, to_l = (w, right), (w, left)
    head, rest = pl.ds(0, LEFT_PART), pl.ds(LEFT_PART, SENT - LEFT_PART)

    def own_right(k):
        block = gathered.at[k, g]
        return remote(block, block, ag_send.at[0, k], ag_recv.at[0, k], to_r)

    def own_left(k):
        block = gathered.at[k, g]
        return remote(block, block, ag_send.at[1, k], ag_recv.at[1, k], to_l)

    def pass_right(k):
        block = gathered.at[k, left, head]
        return remote(block, block, ag_send.at[2, k], ag_recv.at[2, k], to_r)

    def pass_left(k):
        block = gathered.at[k, right, rest]
        return remote(block, block, ag_send.at[3, k], ag_recv.at[3, k], to_l)

    def sum_first_right(k):
        return remote(
            opposite.at[k, head], first_left.at[k], rs_send.at[0, k], rs_recv.at[0, k], to_r
        )

    def sum_first_left(k):
        return remote(
            opposite.at[k, rest], first_right.at[k], rs_send.at[1, k], rs_recv.at[1, k], to_l
        )

    def sum_second_right(k):
        return remote(to_right.at[k], second_left.at[k], rs_send.at[2, k], rs_recv.at[2, k], to_r)

    def sum_second_left(k):
        return remote(to_left.at[k], second_right.at[k], rs_send.at[3, k], rs_recv.at[3, k], to_l)

    def exchange_all(k, count, src, dst, send, recv):
        some, others = pl.ds(k, count), pl.ds(0, WAVE - 1)
        return remote(src.at[some, others], dst.at[some, others], send.at[k], recv.at[k], (w, g))

    z, x, core = w // 8, lax.rem(w // 2, 4), lax.rem(w, 2)

    def exchange(k, count, src, dst, send, recv):
        some = pl.ds(k, count)
        for dz, dx, dc in OTHERS:
            to = lax.rem(z + dz, 4) * 8 + lax.rem(x + dx, 4) * 2 + lax.rem(core + dc, 2)
            remote(src.at[some, to], dst.at[some, w], send.at[k], recv.at[k], (to, g)).start()
        for n in range(count):
            dst[k + n, w] = src[k + n, w]

    for k in range(CHUNKS):
        spec_copy(k).start()
    fixed_copy.start()
    for k in range(CHUNKS):
        leg_copy(k).start()
    barrier = pltpu.get_barrier_semaphore()

    def greet(d, carry):
        pl.semaphore_signal(
            barrier, inc=1, device_id=(lax.rem(w + d, WAVE), g), device_id_type=MESH
        )
        return carry

    for to in (to_r, to_l):
        pl.semaphore_signal(barrier, inc=1, device_id=to, device_id_type=MESH)
    lax.fori_loop(1, WAVE, greet, 0)

    lane = lax.broadcasted_iota(I32, (ROWS, LANES), 1)
    pair_of_row = lax.broadcasted_iota(I32, (ROWS, LANES), 0) & (PAIRS - 1)

    def reverse(values):
        places = [lax.broadcasted_iota(I32, (LANES, LANES), dim) for dim in range(2)]
        flip = (places[0] + places[1] == LANES - 1).astype(F32)
        if values.dtype == BF16:
            return jnp.dot(values, flip.astype(BF16), preferred_element_type=F32)
        return jnp.dot(
            values, flip, precision=lax.Precision.HIGHEST, preferred_element_type=F32
        )

    def fold(spare, s):
        value = jnp.sum(jnp.where(lane == LANES - 1 - s, spare, 0.0), axis=1, keepdims=True)
        value = jnp.broadcast_to(value, (ROWS, LANES))
        spot = lane[:16]
        out = jnp.zeros((16, LANES), F32)
        for n in range(ROWS // 16):
            out = jnp.where(spot == n, value[16 * n : 16 * (n + 1)], out)
        return out

    def unfold(extras):
        spot = lane[:16]
        return jnp.concatenate(
            [
                jnp.broadcast_to(
                    jnp.sum(jnp.where(spot == n, extras, 0.0), axis=1, keepdims=True), (16, LANES)
                )
                for n in range(ROWS // 16)
            ],
            axis=0,
        )

    def recover(blocks, extras, m, kind):
        q, s = m >> 7, m & (LANES - 1)
        shared = blocks[0]
        for t in range(1, NB):
            shared = jnp.where(q == t, blocks[t], shared)
        back_again = reverse(shared.astype(kind))
        spot = LANES - 1 - s
        return jnp.where(lane > spot, back_again, jnp.where(lane == spot, unfold(extras), 0.0))

    def pack(k):
        first_row = (w * CHUNKS + k) * GROUP
        m = jnp.full((ROWS, LANES), own_ref[first_row], I32)
        for i in range(1, PAIRS):
            m = jnp.where(pair_of_row == i, own_ref[first_row + 2 * i], m)
        orders[k] = m
        q = m >> 7
        spec_copy(k).wait()
        for f in range(FD):
            for r in range(GROUP):
                values = spec[k, f, r].astype(F32)
                at = 2 * (f * GROUP + r)
                for t in range(NB):
                    rows[t, at : at + 2, :] = values[:, LANES * t : LANES * (t + 1)]
        first, second = [], []
        for t in range(NB):
            n = lane + LANES * t
            half = [
                jnp.concatenate(
                    [rows[t, pl.ds(2 * ab + c, FD * PAIRS, stride=4), :] for c in range(2)], axis=0
                )
                for ab in range(2)
            ]
            first.append(jnp.where(n >= m, half[0], 0.0))
            second.append(jnp.where(n >= M - 1 - m, half[1], 0.0))
        s = m & (LANES - 1)
        spare = second[NB - 1]
        for t in range(1, NB):
            spare = jnp.where(q == t, second[NB - 1 - t], spare)
        turned_round = reverse(spare.astype(BF16))
        for t in range(NB):
            shared = jnp.where(lane >= s, first[t], turned_round)
            block = jnp.where(q < t, first[t], jnp.where(q == t, shared, second[NB - 1 - t]))
            gathered[k, g, ROWS * t : ROWS * (t + 1), :] = block.astype(BF16)
        gathered[k, g, NB * ROWS :, :] = fold(spare, s).astype(BF16)

    def first_pack(k, carry):
        pack(k)

        @pl.when(k == 0)
        def _():
            pl.semaphore_wait(barrier, WAVE + 1)
            own_right(0).start()
            own_left(0).start()

        return carry

    lax.fori_loop(0, 2, first_pack, 0)

    spot = lax.broadcasted_iota(I32, (1, LANES), 1)
    lat_of = lambda x: sum((x >= FL * n).astype(I32) for n in range(1, LATS))
    level_of = lambda x: x - FL * lat_of(x)
    length, weight = jnp.zeros((1, LANES), I32), jnp.zeros((1, LANES), F32)
    for lat in range(LATS):
        at = (g * LATS + lat) * WAVE + w
        length = jnp.where(spot >= FL * lat, lengths_ref[at], length)
        weight = jnp.where(spot >= FL * lat, weights_ref[at], weight)
    gain = jnp.zeros((1, LANES), F32)
    for f in range(FL):
        gain = jnp.where(level_of(spot) == f, gains_ref[f], gain)
    gain = jnp.concatenate([gain, gain], axis=1)
    real_length = length.astype(F32)
    root = lax.rsqrt(real_length)
    scale = weight * (root * (1.5 - 0.5 * real_length * root * root))
    half_length = length >> 1
    inverse_length = 1.0 / real_length
    count = length >> 9

    spot = lax.broadcasted_iota(I32, (FL, LANES), 1)
    level = lax.broadcasted_iota(I32, (FL, LANES), 0)
    hot = ((level_of(spot) == level) & (spot < LATS * FL)).astype(F32)
    across_levels = (((0,), (0,)), ((), ()))
    spread = lax.dot_general(
        mixing_ref[...], hot, across_levels, precision=lax.Precision.HIGHEST,
        preferred_element_type=F32,
    )
    spread = lax.dot_general(
        hot, spread, across_levels, precision=lax.Precision.HIGHEST, preferred_element_type=F32
    )
    lats = [lat_of(lax.broadcasted_iota(I32, (LANES, LANES), dim)) for dim in range(2)]
    spread = jnp.where(lats[0] == lats[1], spread, 0.0)
    high_part = spread.astype(BF16)
    mix_ref[:LANES] = high_part
    mix_ref[LANES:] = (spread - high_part.astype(F32)).astype(BF16)

    width = WAVE * GROUP

    def tables(k):
        spot = lax.broadcasted_iota(I32, (width, LANES), 1)
        row = lax.broadcasted_iota(I32, (width, LANES), 0)
        row = (row >> 3) * (CHUNKS * GROUP) + k * GROUP + (row & 7)
        m = jnp.broadcast_to(order_ref[0:1, :], (width, LANES))
        for n in range(1, NB):
            m = jnp.where((row >> 7) == n, order_ref[n : n + 1, :], m)
        m = jnp.where(spot == (row & 127), m, 0).astype(F32)
        m = jnp.broadcast_to(jnp.sum(m, axis=1, keepdims=True), (width, LANES))
        across_lanes = m.T[0:1, :].astype(I32)
        m = m.astype(I32)
        column_orders[k] = m
        t = jnp.where(m < half_length, m.astype(F32) * inverse_length, 0.0)
        tr[k], ti[k] = turn_pair(t)

        spot = lax.broadcasted_iota(I32, (width, BLOCK), 1)
        m = jnp.concatenate([m & (BLOCK - 1)] * (BLOCK // LANES), axis=1)
        hot = (spot == m).astype(F32).astype(BF16)
        for half in range(2):
            table[k, half * width : (half + 1) * width] = jnp.dot(
                hot, base_ref[:, half * BLOCK : half * BLOCK + HALF], preferred_element_type=F32
            ).astype(BF16)
        spot = lax.broadcasted_iota(I32, (BLOCK, width), 0)
        hot = (spot == (across_lanes & (BLOCK - 1))).astype(F32).astype(BF16)
        turned[k, :EVEN] = jnp.dot(
            base_ref[:EVEN, :BLOCK], hot, preferred_element_type=F32
        ).astype(BF16)
        turned[k, EVEN:] = jnp.dot(
            base_ref[:HALF, BLOCK:], hot, preferred_element_type=F32
        ).astype(BF16)

    fixed_copy.wait()
    side = 2 * LANES
    for n in range(4):
        base_ref[:, side * n : side * (n + 1)] = grid[n, :BLOCK].astype(BF16)
    for n in range(2):
        pick_ref[:, side * n : side * (n + 1)] = grid[4 + n, :BLOCK].astype(BF16)
        turn_ref[side * n : side * (n + 1), :] = grid[4 + n, :BLOCK].T.astype(BF16)
    for s in range(XMAX // 2):
        grid[s] = jnp.zeros((EVEN + HALF, side), F32)

    def pack_legendre(k):
        for i in range(PAIRS):
            load_packed(legs, packed.at[i], GROUP * k + 2 * i, orders[k, i : i + 1, :] >> 7)

    def spread_group(k, d):
        group = pl.ds(pl.multiple_of(d * ROWS, 16), ROWS)
        blocks = []
        for t in range(NB):
            blocks.append(gathered[k, d, ROWS * t : ROWS * (t + 1), :].astype(F32))
            coeff[t, group, :] = blocks[t]
        extras = gathered[k, d, NB * ROWS :, :].astype(F32)
        coeff[NB, group, :] = recover(blocks, extras, orders[k], BF16)

    def legendre_sum(k):
        spread_group(k, across)
        for i in range(PAIRS):
            m = orders[k, i : i + 1, :]
            q = m >> 7
            spot = lax.broadcasted_iota(I32, (1, LANES), 1)
            weights = []
            for t in range(PB):
                block = coeff[t, pl.ds(i, ROWS, stride=PAIRS), :]
                if t < NB:
                    lead = jnp.where(spot + LANES * t >= m, block, 0.0)
                    other = jnp.where(q > t, block, 0.0)
                else:
                    lead, other = jnp.zeros_like(block), block
                weights.append(
                    jnp.concatenate([lead, other, jnp.zeros((32, LANES), F32)], axis=0).astype(BF16)
                )
            fourier = lax.dot_general(
                packed[i],
                jnp.concatenate(weights, axis=1),
                (((1,), (1,)), ((), ())),
                preferred_element_type=F32,
            ).astype(BF16)
            for lat in range(LATS):
                wide[WAVE * i : WAVE * (i + 1), LANES * lat : LANES * (lat + 1)] = fourier[
                    WAVE * lat : WAVE * (lat + 1)
                ]
        placed = jnp.dot(wide[...], turn_ref[...], preferred_element_type=F32)
        for c in range(2):
            for ab in range(2):
                for i in range(PAIRS):
                    at = 2 * c + ab
                    turn[pl.ds(c * 8 + 2 * i + ab, WAVE, stride=16), :] = placed[
                        WAVE * i : WAVE * (i + 1), LANES * at : LANES * (at + 1)
                    ]
        sent[k] = turn[...].reshape(WAVE, 16, LANES).astype(BF16)

    def grid_sum(k, last):
        keep = column_orders[k] < half_length
        one = tr[k], ti[k]
        two = times(one, one)
        four = times(two, two)
        eight = times(four, four)
        eleven = times(times(eight, two), one)
        x = arrived[k].astype(F32)
        x = jnp.concatenate(
            [x[:, :8].reshape(width, LANES), x[:, 8:].reshape(width, LANES)], axis=0
        ).astype(BF16)
        x = jnp.dot(
            jnp.concatenate([x, x], axis=1), mix_ref[...], preferred_element_type=F32
        )
        x0 = jnp.where(keep, x[:width], 0.0)
        x1 = jnp.where(keep, x[width:], 0.0)
        h = times((x0, x1), eleven)
        for s in range(XMAX // 2):
            for side in range(2):
                span = slice(LANES * side, LANES * (side + 1))
                waves[s, :width, span] = h[0].astype(BF16)
                waves[s, width:, span] = h[1].astype(BF16)
                h = back(h, one)
        for s in range(XMAX // 2):
            even = grid[s, :EVEN] + jnp.dot(
                turned[k, :EVEN], waves[s, :width], preferred_element_type=F32
            )
            odd = grid[s, EVEN:] + jnp.dot(
                turned[k, EVEN:], waves[s, width:], preferred_element_type=F32
            )
            if not last:
                grid[s, :EVEN] = even
                grid[s, EVEN:] = odd
                continue
            high = XMAX - 1 - 2 * s
            live = jnp.concatenate(
                [(high < count).astype(F32), (high - 1 < count).astype(F32)], axis=1
            )

            def column(values):
                mixed = values * float(M) ** (-0.5)
                return (mixed + gain * mixed * mixed) * live

            one = column(even[:HALF] + odd)
            two = column(even[:HALF] - odd)
            two = jnp.where(lax.broadcasted_iota(I32, two.shape, 0) == 0, 0.0, two)
            update[s, :HALF] = (one + two).astype(BF16)
            update[s, HALF:] = (one - two).astype(BF16)
            edge[s] = column(even[HALF : HALF + 8])

    own_right(1).start()
    own_left(1).start()
    pack(2)
    tables(0)

    def some_tables(k, carry):
        tables(k)
        return carry

    def gather_step(k, carry):
        @pl.when(k < CHUNKS)
        def _():
            own_right(k).wait_recv()
            pass_right(k).start()
            own_left(k).wait_recv()
            pass_left(k).start()

        @pl.when(k + 3 < CHUNKS)
        def _():
            pack(k + 3)
            lax.fori_loop(2 * k + 1, 2 * k + 3, some_tables, 0)

        @pl.when(k + 2 < CHUNKS)
        def _():
            own_right(k + 2).start()
            own_left(k + 2).start()

        @pl.when((k >= 1) & (k <= CHUNKS))
        def _():
            leg_copy(k - 1).wait()
            pack_legendre(k - 1)
            for d in (g, left, right):
                spread_group(k - 1, d)
            pass_right(k - 1).wait_recv()
            pass_left(k - 1).wait_recv()
            legendre_sum(k - 1)

        @pl.when(k == 2)
        def _():
            exchange(0, 2, sent, arrived, a_send, a_recv)

        @pl.when(k >= 3)
        def _():
            exchange(k - 1, 1, sent, arrived, a_send, a_recv)

        @pl.when(k == 3)
        def _():
            exchange_all(0, 2, sent, arrived, a_send, a_recv).wait_recv()

        @pl.when(k == 4)
        def _():
            grid_sum(0, False)

        return carry

    lax.fori_loop(0, CHUNKS + 1, gather_step, 0)

    def late_sum(k, carry):
        @pl.when(k >= 2)
        def _():
            exchange_all(k, 1, sent, arrived, a_send, a_recv).wait_recv()

        grid_sum(k, False)
        return carry

    lax.fori_loop(1, CHUNKS - 1, late_sum, 0)
    exchange_all(CHUNKS - 1, 1, sent, arrived, a_send, a_recv).wait_recv()
    grid_sum(CHUNKS - 1, True)

    def grid_back(k):
        t = tr[k], ti[k]
        d = jnp.zeros((width, LANES), F32), jnp.zeros((width, LANES), F32)
        sign = 1.0 - 2.0 * (column_orders[k] & 1).astype(F32)
        for s in range(XMAX // 2):
            even = jnp.dot(table[k, :width], update[s, :HALF], preferred_element_type=F32)
            odd = jnp.dot(table[k, width:], update[s, HALF:], preferred_element_type=F32)
            for side in range(2):
                span = slice(LANES * side, LANES * (side + 1))
                if s + side > 0:
                    d = back(d, t)
                d = d[0] + (even[:, span] + sign * edge[s, 0:1, span]), d[1] + odd[:, span]
        keep = column_orders[k] < half_length
        d0 = jnp.where(keep, d[0] * scale, 0.0).reshape(WAVE, 8, LANES)
        d1 = jnp.where(keep, d[1] * scale, 0.0).reshape(WAVE, 8, LANES)
        sent_back[k] = jnp.concatenate([d0, d1], axis=1).astype(BF16)

    def legendre_back(k):
        turn[...] = arrived_back[k].reshape(WAVE * 16, LANES).astype(F32)
        for c in range(2):
            for ab in range(2):
                for i in range(PAIRS):
                    at = 2 * c + ab
                    wide[WAVE * i : WAVE * (i + 1), LANES * at : LANES * (at + 1)] = turn[
                        pl.ds(c * 8 + 2 * i + ab, WAVE, stride=16), :
                    ].astype(BF16)
        spread = jnp.dot(wide[...], pick_ref[...], preferred_element_type=F32)
        for i in range(PAIRS):
            q = orders[k, i : i + 1, :] >> 7
            values = jnp.concatenate(
                [
                    spread[WAVE * i : WAVE * (i + 1), LANES * lat : LANES * (lat + 1)]
                    for lat in range(LATS)
                ],
                axis=0,
            )
            values = values.T.astype(BF16)
            result = jnp.dot(values[: 2 * ROWS], packed[i], preferred_element_type=F32)
            for t in range(PB):
                span = slice(LANES * t, LANES * (t + 1))
                if t < NB:
                    block = jnp.where(q <= t, result[:ROWS, span], result[ROWS:, span])
                else:
                    block = result[ROWS:, span]
                coeff[t, pl.ds(i, ROWS, stride=PAIRS), :] = block
        m = orders[k]
        q, s = m >> 7, m & (LANES - 1)
        flipped[...] = reverse(coeff[NB].astype(BF16))
        own_rows = lambda d: pl.ds(pl.multiple_of(d * ROWS, 16), ROWS)
        places = (
            (opposite, across, BF16), (part_right, right, F32), (part_left, left, F32), (part_own, g, F32)
        )
        for place, d, kind in places:
            for t in range(NB):
                shared = (q == t) & (lane < s)
                block = jnp.where(shared, flipped[own_rows(d), :], coeff[t, own_rows(d), :])
                place[k, ROWS * t : ROWS * (t + 1), :] = block.astype(kind)
            place[k, NB * ROWS :, :] = fold(coeff[NB, own_rows(d), :], s).astype(kind)
            if place is opposite:
                sum_first_right(k).start()
                sum_first_left(k).start()

    def sum_second(k):
        cut = LEFT_PART
        to_right[k, :cut] = (part_right[k, :cut] + first_left[k].astype(F32)).astype(BF16)
        to_right[k, cut:] = part_right[k, cut:].astype(BF16)
        sum_second_right(k).start()
        sum_first_left(k).wait_recv()
        to_left[k, :cut] = part_left[k, :cut].astype(BF16)
        to_left[k, cut:] = (part_left[k, cut:] + first_right[k].astype(F32)).astype(BF16)
        sum_second_left(k).start()

    def unpack(k):
        m = orders[k]
        q = m >> 7
        whole = lambda at: (
            part_own[k, at, :] + second_left[k, at, :].astype(F32) + second_right[k, at, :].astype(F32)
        )
        total = [whole(slice(ROWS * t, ROWS * (t + 1))) for t in range(NB)]
        total.append(recover(total, whole(slice(NB * ROWS, SENT)), m, F32))
        for t in range(NB):
            n = lane + LANES * t
            other = jnp.where(NB - 1 - t == q, total[NB], total[NB - 1 - t])
            both = jnp.where(n >= m, total[t], 0.0), jnp.where(n >= M - 1 - m, other, 0.0)
            count = FD * PAIRS
            for ab in range(2):
                for c in range(2):
                    rows[t, pl.ds(2 * ab + c, count, stride=4), :] = both[ab][count * c : count * (c + 1)]
        for f in range(FD):
            for r in range(GROUP):
                at = 2 * (f * GROUP + r)
                results[k, f, r] = jnp.concatenate(
                    [rows[t, at : at + 2, :] for t in range(NB)], axis=1
                )

    def back_step(k):
        grid_back(k)
        exchange(k, 1, sent_back, arrived_back, b_send, b_recv)

    def ahead(k, carry):
        back_step(k)
        return carry

    lax.fori_loop(0, 3, ahead, 0)

    def scatter_step(k, carry):
        @pl.when(k < CHUNKS)
        def _():
            pack_legendre(k)
            exchange_all(k, 1, sent_back, arrived_back, b_send, b_recv).wait_recv()
            legendre_back(k)

        @pl.when((k >= 1) & (k <= CHUNKS))
        def _():
            sum_first_right(k - 1).wait_recv()
            sum_second(k - 1)

        @pl.when((k >= 1) & (k + 2 < CHUNKS))
        def _():
            back_step(k + 2)

        @pl.when(k >= 4)
        def _():
            sum_second_right(k - 4).wait_recv()
            sum_second_left(k - 4).wait_recv()
            unpack(k - 4)
            out_copy(k - 4).start()

        return carry

    lax.fori_loop(0, CHUNKS + 4, scatter_step, 0)

    def finish(k, carry):
        for copy in (own_right, own_left, pass_right, pass_left):
            copy(k).wait_send()
        for copy in (sum_first_right, sum_first_left, sum_second_right, sum_second_left):
            copy(k).wait_send()
        exchange_all(k, 1, sent_back, arrived_back, b_send, b_recv).wait_send()
        out_copy(k).wait()
        return carry

    lax.fori_loop(0, CHUNKS, finish, 0)
    for k, count in ((0, 2), (2, 1), (3, 1), (4, 1)):
        exchange_all(k, count, sent, arrived, a_send, a_recv).wait_send()


PIECES = 5


def hand_over(src_ref, dst_ref, held, sem_in, sem_out):
    count = src_ref.shape[1] // PIECES
    spans = [pl.ds(n * count, count) for n in range(PIECES)]
    reads = [
        pltpu.make_async_copy(src_ref.at[:, at], held.at[:, at], sem_in.at[n])
        for n, at in enumerate(spans)
    ]
    writes = [
        pltpu.make_async_copy(held.at[:, at], dst_ref.at[:, at], sem_out.at[n])
        for n, at in enumerate(spans)
    ]
    for read in reads:
        read.start()
    for read, write in zip(reads, writes):
        read.wait()
        write.start()
    for write in writes:
        write.wait()


VMEM = pl.BlockSpec(memory_space=pltpu.VMEM)
SMEM = pl.BlockSpec(memory_space=pltpu.SMEM)
ANY = pl.BlockSpec(memory_space=pl.ANY)


def local(spec_in, legendre, wave_order, row_length, quad_weight, mixing, square_gain):
    fixed = np.concatenate([wave_tables(), lane_maps()], axis=1)
    fixed = fixed.reshape(BLOCK, XMAX // 2, 2 * LANES).transpose(1, 0, 2)
    width = WAVE * GROUP
    message = pltpu.VMEM((CHUNKS, WAVE, 16, LANES), BF16)
    full = pltpu.VMEM((CHUNKS, SENT, LANES), F32)
    short = pltpu.VMEM((CHUNKS, SENT, LANES), BF16)
    turns = pltpu.VMEM((CHUNKS, width, LANES), F32)
    places = pltpu.VMEM((LATS * LANES, LATS * LANES), BF16)
    copies = pltpu.SemaphoreType.DMA((4, CHUNKS))
    each = pltpu.SemaphoreType.DMA((CHUNKS,))
    result = pl.pallas_call(
        kernel,
        out_shape=jax.ShapeDtypeStruct((FD, GROUP * CHUNKS, 2, M), F32),
        in_specs=[ANY] * 3 + [SMEM] * 4 + [VMEM] * 2,
        out_specs=ANY,
        scratch_shapes=[
            pltpu.VMEM((GROUP * CHUNKS, FLD * WAVE, M), BF16),
            pltpu.VMEM((BLOCK, 2 * BLOCK), BF16),
            places,
            places,
            pltpu.VMEM((CHUNKS, FD, GROUP, 2, M), BF16),
            pltpu.VMEM((NB, 2 * ROWS, LANES), F32),
            pltpu.VMEM((CHUNKS, ROWS, LANES), I32),
            pltpu.VMEM((2 * LANES, LANES), BF16),
            pltpu.VMEM((CHUNKS, width, LANES), I32),
            pltpu.VMEM((CHUNKS, FLD, SENT, LANES), BF16),
            pltpu.VMEM((PB, FLD * ROWS, LANES), F32),
            pltpu.VMEM((FLD * ROWS, LANES), F32),
            pltpu.VMEM((PAIRS, LANES, PACKED), BF16),
            pltpu.VMEM((PAIRS * WAVE, LATS * LANES), BF16),
            pltpu.VMEM((WAVE * 16, LANES), F32),
            message,
            message,
            pltpu.VMEM((CHUNKS, 2 * width, HALF), BF16),
            pltpu.VMEM((CHUNKS, EVEN + HALF, width), BF16),
            pltpu.VMEM((XMAX // 2, 2 * width, 2 * LANES), BF16),
            pltpu.VMEM((XMAX // 2, EVEN + HALF, 2 * LANES), F32),
            pltpu.VMEM((XMAX // 2, BLOCK, 2 * LANES), BF16),
            pltpu.VMEM((XMAX // 2, 8, 2 * LANES), F32),
            turns,
            turns,
            message,
            message,
            short,
            full,
            full,
            full,
            short,
            short,
            pltpu.VMEM((CHUNKS, LEFT_PART, LANES), BF16),
            pltpu.VMEM((CHUNKS, SENT - LEFT_PART, LANES), BF16),
            short,
            short,
            pltpu.VMEM((CHUNKS, FD, GROUP, 2, M), F32),
            each,
            each,
            pltpu.SemaphoreType.DMA,
            each,
            copies,
            copies,
            each,
            each,
            each,
            each,
            copies,
            copies,
        ],
        compiler_params=pltpu.CompilerParams(
            collective_id=0, has_side_effects=True, vmem_limit_bytes=60 << 20
        ),
    )(
        spec_in, legendre, jnp.asarray(fixed),
        wave_order, row_length, quad_weight, square_gain,
        wave_order.reshape(NB, LANES), mixing,
    )
    return pl.pallas_call(
        hand_over,
        out_shape=jax.ShapeDtypeStruct(result.shape, F32),
        in_specs=[ANY],
        out_specs=ANY,
        scratch_shapes=[
            pltpu.VMEM(result.shape, F32),
            pltpu.SemaphoreType.DMA((PIECES,)),
            pltpu.SemaphoreType.DMA((PIECES,)),
        ],
        compiler_params=pltpu.CompilerParams(vmem_limit_bytes=60 << 20),
    )(result)

def solution(mesh):
    in_specs = (P("fld", "wave", None, None), P("wave", "fld", None), P(), P(), P(), P(), P())
    out_specs = P("fld", "wave", None, None)
    return jax.shard_map(local, mesh=mesh, in_specs=in_specs, out_specs=out_specs, check_vma=False)
```

profile of v0, /device:TPU:1, one launch (start us, length us, event | category | flops | bytes accessed | tf_op | source)
XLA Modules:
  0.0 77.3 jit_solution(11649582031433494955)
XLA Ops:
  0.0 74.7 %shard_map.82.src_ref = f32[6,40,2,1280]{3,2,1,0:T(2,128)} custom-call(bf16[6,40,2,1280]{3,2,1,0:T(2,128)(2,1)} %spec_ref.1, bf16[40,128,1280]{2,1,0:T(8,128)(2,1)} %leg_ref.1, f32[6,512,256]{2,1,0:T(8,128)} %constant.2.clone.fixed_ref, s32[1280]{0:T(1024)} %own_ref.1, s32[512]{0:T(512)} %lengths_ref.1, f32[512]{0:T(512)} %weights_ref.1, f32[24]{0:T(128)} %gains_ref.1, ...), custom_call_target="tpu_custom_call" | custom-call | tf_op jit(solution)/shard_map/pallas_call | solution.py:741
  74.7 2.5 %shard_map.83 = f32[6,40,2,1280]{3,2,1,0:T(2,128)} custom-call(f32[6,40,2,1280]{3,2,1,0:T(2,128)} %shard_map.82.src_ref), custom_call_target="tpu_custom_call" | custom-call | tf_op jit(solution)/shard_map/pallas_call | solution.py:806
where the time goes:
time: 77.5 us; the launch traced here: 77.3 us
  Pallas kernels  77.3 us (100%)
    pallas_call x1, Pallas kernels, local(): pl.pallas_call(kernel, out_shape=jax.ShapeDtypeStruct((FD, GROUP * CHUNKS...  74.7 us
    pallas_call x1, Pallas kernels, local(): pl.pallas_call(hand_over, out_shape=jax.ShapeDtypeStruct(result.shape, F3...  2.54 us

commit v1 on v0

--- a/solution.py
+++ b/solution.py
@@ -374,6 +374,7 @@
             base_ref[:HALF, BLOCK:], hot, preferred_element_type=F32
         ).astype(BF16)
 
+    waves[0, :, :LANES] = jnp.zeros((2 * width, LANES), BF16)
     fixed_copy.wait()
     side = 2 * LANES
     for n in range(4):
@@ -440,7 +441,7 @@
         two = times(one, one)
         four = times(two, two)
         eight = times(four, four)
-        eleven = times(times(eight, two), one)
+        ten = times(eight, two)
         x = arrived[k].astype(F32)
         x = jnp.concatenate(
             [x[:, :8].reshape(width, LANES), x[:, 8:].reshape(width, LANES)], axis=0
@@ -450,9 +451,9 @@
         )
         x0 = jnp.where(keep, x[:width], 0.0)
         x1 = jnp.where(keep, x[width:], 0.0)
-        h = times((x0, x1), eleven)
+        h = times((x0, x1), ten)
         for s in range(XMAX // 2):
-            for side in range(2):
+            for side in range(0 if s else 1, 2):
                 span = slice(LANES * side, LANES * (side + 1))
                 waves[s, :width, span] = h[0].astype(BF16)
                 waves[s, width:, span] = h[1].astype(BF16)
@@ -560,9 +561,9 @@
         for s in range(XMAX // 2):
             even = jnp.dot(table[k, :width], update[s, :HALF], preferred_element_type=F32)
             odd = jnp.dot(table[k, width:], update[s, HALF:], preferred_element_type=F32)
-            for side in range(2):
+            for side in range(0 if s else 1, 2):
                 span = slice(LANES * side, LANES * (side + 1))
-                if s + side > 0:
+                if s > 0:
                     d = back(d, t)
                 d = d[0] + (even[:, span] + sign * edge[s, 0:1, span]), d[1] + odd[:, span]
         keep = column_orders[k] < half_length

time: 77.5 us -> 77.4 us (level)
  no operation moved by 1% of the time
where the time goes in v1:
time: 77.4 us; the launch traced here: 77.2 us
  Pallas kernels  77.2 us (100%)
    pallas_call x1, Pallas kernels, local(): pl.pallas_call(kernel, out_shape=jax.ShapeDtypeStruct((FD, GROUP * CHUNKS...  74.6 us
    pallas_call x1, Pallas kernels, local(): pl.pallas_call(hand_over, out_shape=jax.ShapeDtypeStruct(result.shape, F3...  2.54 us

profile of v1, /device:TPU:1, one launch (start us, length us, event | category | flops | bytes accessed | tf_op | source)
XLA Modules:
  0.0 77.2 jit_solution(13700831510624169494)
XLA Ops:
  0.0 74.6 %shard_map.82.src_ref = f32[6,40,2,1280]{3,2,1,0:T(2,128)} custom-call(bf16[6,40,2,1280]{3,2,1,0:T(2,128)(2,1)} %spec_ref.1, bf16[40,128,1280]{2,1,0:T(8,128)(2,1)} %leg_ref.1, f32[6,512,256]{2,1,0:T(8,128)} %constant.2.clone.fixed_ref, s32[1280]{0:T(1024)} %own_ref.1, s32[512]{0:T(512)} %lengths_ref.1, f32[512]{0:T(512)} %weights_ref.1, f32[24]{0:T(128)} %gains_ref.1, ...), custom_call_target="tpu_custom_call" | custom-call | tf_op jit(solution)/shard_map/pallas_call | solution.py:742
  74.6 2.5 %shard_map.83 = f32[6,40,2,1280]{3,2,1,0:T(2,128)} custom-call(f32[6,40,2,1280]{3,2,1,0:T(2,128)} %shard_map.82.src_ref), custom_call_target="tpu_custom_call" | custom-call | tf_op jit(solution)/shard_map/pallas_call | solution.py:807
